TPU v7x, 512 devices: a whole 4x8x8 slice. The times are simulated.
512 devices in a mesh: users: 128 (over z, y, core), heads: 4 (over x).
Axes of the slice: x: 4, y: 8, z: 8, core: 2. Of those that a mesh axis runs over, the one named last changes fastest.
Arguments:
- history: bfloat16 [128, 4096, 512], P('users'), may hold values from -6 to 6
- candidates: bfloat16 [128, 1024, 512], P('users'), may hold values from -70 to 70
- lengths: int32 [128], replicated, may hold values from 512 to 4096, as said below
- counts: int32 [128], replicated, may hold values from 128 to 1024, as said below
- w_query: bfloat16 [512, 512], P(None, 'heads'), may hold values from -0.25 to 0.25
- w_key: bfloat16 [512, 512], P(None, 'heads'), may hold values from -0.25 to 0.25
- w_value: bfloat16 [512, 512], P(None, 'heads'), may hold values from -0.25 to 0.25
- w_out: bfloat16 [512, 512], P('heads'), may hold values from -0.375 to 0.375
Outputs:
- mixed: float32 [128, 1024, 512], P('users', None, 'heads')
Inputs may be any that keep to these rules, and one draw needn't show every extreme that they name: `lengths`: one user has exactly 4096 events. `counts`: one user has exactly 1024 candidates.
All inputs are finite; a program needn't handle non-finite values.
Results may differ from a plain program's by a relative error of at most 0.0085.
The roundings to bfloat16 on the way count: a program that leaves them out, or rounds other values in their place, can miss the bound.
Values may be sent and summed in bfloat16 or wider, within the bound.
A program may use at most 128 MiB of HBM per device.

v0:
```python
import jax
import jax.numpy as jnp
from jax import lax
from jax.sharding import PartitionSpec as P

D = 512
HD = 64
CH = 256
LMAX = 4096
CMAX = 1024


def swapped(block, axis, apart):
    count = lax.axis_size(axis)
    route = []
    for low in range(count):
        high = low | 1 << apart
        if high != low and high < count:
            route += [(low, high), (high, low)]
    return lax.ppermute(block, axis, route)


def empty_state(head_count):
    return (
        jnp.full((head_count, CMAX), -1e30, jnp.float32),
        jnp.zeros((head_count, CMAX), jnp.float32),
        jnp.zeros((head_count, CMAX, HD), jnp.float32),
    )


def absorb(state, block, place, length, query, kv_weight):
    run_max, run_total, run_sum = state
    head_count = query.shape[1]
    projected = jnp.dot(block, kv_weight, preferred_element_type=jnp.float32).astype(jnp.bfloat16)
    projected = projected.reshape(CH, 2, head_count, HD)
    score = jnp.einsum("chd,khd->hck", query, projected[:, 0], preferred_element_type=jnp.float32)
    position = place * CH + jnp.arange(CH, dtype=jnp.int32)
    score = jnp.where((position < length)[None, None, :], score, -jnp.inf)
    new_max = jnp.maximum(run_max, jnp.max(score, axis=-1))
    weight = jnp.exp(score - new_max[..., None])
    factor = jnp.exp(run_max - new_max)
    new_total = run_total * factor + jnp.sum(weight, axis=-1)
    product = jnp.einsum(
        "hck,khd->hcd",
        weight.astype(jnp.bfloat16),
        projected[:, 1],
        preferred_element_type=jnp.float32,
    )
    return (new_max, new_total, run_sum * factor[..., None] + product)


def attend(
    blocks, local_stride, local_start, global_stride, global_start, length, query, kv_weight
):
    block_total = (length + CH - 1) // CH
    steps_needed = jnp.maximum((block_total - global_start + global_stride - 1) // global_stride, 0)

    def advance(step, state):
        local = step * local_stride + local_start
        place = step * global_stride + global_start
        block = lax.dynamic_index_in_dim(blocks, local, 0, keepdims=False)
        return absorb(state, block, place, length, query, kv_weight)

    return lax.fori_loop(0, steps_needed, advance, empty_state(query.shape[1]))


def combine_states(first, second):
    top = jnp.maximum(first[0], second[0])
    left = jnp.exp(first[0] - top)
    right = jnp.exp(second[0] - top)
    total = first[1] * left + second[1] * right
    summed = first[2] * left[..., None] + second[2] * right[..., None]
    return (top, total, summed)


def body(history, candidates, lengths, counts, w_query, w_key, w_value, w_out):
    head_count = w_out.shape[0] // HD
    query = (
        jnp.dot(candidates[0], w_query, preferred_element_type=jnp.float32) * HD ** (-0.5)
    ).astype(jnp.bfloat16)
    query = query.reshape(CMAX, head_count, HD)
    kv_weight = jnp.concatenate([w_key, w_value], axis=1)
    block_count = LMAX // CH
    blocks = history[0].reshape(block_count, CH, D)
    me = lax.axis_index("users")
    own_length = lengths[me]
    bit = lax.axis_size("users").bit_length() - 2
    parity = jnp.right_shift(me, bit) % 2
    partner = jnp.bitwise_xor(me, 1 << bit)
    halves = blocks.reshape(LMAX // (2 * CH), 2, CH, D)
    outgoing = lax.dynamic_index_in_dim(halves, 1 - parity, 1, keepdims=False)
    their_blocks, their_query = swapped((outgoing, query), "users", bit)
    own_state = attend(blocks, 2, parity, 2, parity, own_length, query, kv_weight)
    their_state = attend(their_blocks, 1, 0, 2, parity, lengths[partner], their_query, kv_weight)
    returned = swapped((their_state[0], their_state[1], their_state[2]), "users", bit)
    state = combine_states(own_state, returned)
    attended = (state[2] / state[1][..., None]).astype(jnp.bfloat16)
    rows = w_out.reshape(head_count, HD, D)
    term = jnp.einsum("hcd,hde->ce", attended, rows, preferred_element_type=jnp.float32)
    live = jnp.arange(CMAX, dtype=jnp.int32) < counts[me]
    term = jnp.where(live[:, None], term, jnp.float32(0.0))
    summed = lax.psum_scatter(term[None], "heads", scatter_dimension=2, tiled=True)
    return summed


def solution(mesh):
    placed = (
        P("users", None, None),
        P("users", None, None),
        P(),
        P(),
        P(None, "heads"),
        P(None, "heads"),
        P(None, "heads"),
        P("heads", None),
    )
    return jax.shard_map(
        body, mesh=mesh, in_specs=placed, out_specs=P("users", None, "heads"), check_vma=False
    )
```

profile of v0, /device:TPU:1, one launch (start us, length us, event | category | flops | bytes accessed | tf_op | source)
XLA Modules:
  0.0 243.2 jit_solution(5139779474855725320)
XLA Ops:
  6.6 3.1 %dynamic-slice_bitcast_fusion = bf16[8,256,512]{2,1,0:T(8,128)(2,1)} fusion(bf16[8,2,256,512]{3,2,1,0:T(8,128)(2,1)} %bitcast.112, s32[]{:T(128)S(6)} %select_n.63), kind=kLoop, calls=%fused_computation.42 | loop fusion | bytes 4194308 | tf_op jit(solution)/shard_map/jit(dynamic_index_in_dim)/squeeze | solution.py:91
  9.7 11.5 %collective-permute-start = (bf16[8,256,512]{2,1,0:T(8,128)(2,1)}, bf16[8,256,512]{2,1,0:T(8,128)(2,1)}, u32[]{:S(2)}, u32[]{:S(2)}) collective-permute-start(bf16[8,256,512]{2,1,0:T(8,128)(2,1)} %dynamic-slice_bitcast_fusion), channel_id=1, source_target_pairs={{0,256},{256,0},{4,260},{260,4},{8,264},{264,8},{12,268},{268,12},... | collective-permute-start | bytes 6291464 | tf_op jit(solution)/shard_map/ppermute | solution.py:20
  21.2 0.5 fusion.25
  21.7 1.9 collective-permute-start.1
  23.6 0.7 fusion.34
  25.7 45.9 %collective-permute-done.1 = bf16[1024,2,64]{0,2,1:T(8,128)(2,1)S(1)} collective-permute-done((bf16[1024,2,64]{0,2,1:T(8,128)(2,1)S(1)}, bf16[1024,2,64]{0,2,1:T(8,128)(2,1)S(1)}, u32[]{:S(2)}, u32[]{:S(2)}) %collective-permute-start.1) | collective-permute-done | bytes 262176 | tf_op jit(solution)/shard_map/ppermute | solution.py:20
  71.7 0.0 collective-permute-done
  71.7 3.6 %while.29 = (s32[]{:T(128)}, f32[2,1024]{1,0:T(2,128)S(1)}, f32[2,1024]{1,0:T(2,128)S(1)}, f32[2,1024,64]{1,2,0:T(8,128)S(1)}, s32[]{:T(128)}, /*index=5*/s32[]{...) while((s32[]{:T(128)}, f32[2,1024]{1,0:T(2,128)S(1)}, ...), condition=%wide.region_7.8_spmd, body=%wide.region_4.7_spmd.sunk | while | flops 205853184 | bytes 8521447 | solution.py:64
  71.8 0.7 add_compare_fusion.5
  72.5 1.2 convolution_convert_fusion.5
  73.7 0.5 bitcast_reduce_fusion.5
  74.2 0.4 fusion.60
  74.7 0.6 convolution_add_fusion.5
  75.4 8.0 %collective-permute-start.3 = (f32[2,1024,64]{1,2,0:T(8,128)S(1)}, f32[2,1024,64]{1,2,0:T(8,128)S(1)}, u32[]{:S(2)}, u32[]{:S(2)}) collective-permute-start(f32[2,1024,64]{1,2,0:T(8,128)S(1)} %get-tuple-element.118), channel_id=1, source_target_pairs={{0,256},{256,0},{4,260},{260,4},{8,264},{264,8},{12,268},{268,12},... | collective-permute-start | bytes 1572872 | tf_op jit(solution)/shard_map/ppermute | solution.py:20
  83.5 0.0 copy-start.6
  83.5 0.0 copy-start.5
  83.5 3.5 %while.28 = (s32[]{:T(128)}, f32[2,1024]{1,0:T(2,128)S(1)}, f32[2,1024]{1,0:T(2,128)S(1)}, f32[2,1024,64]{1,2,0:T(8,128)S(1)}, s32[]{:T(128)}, /*index=5*/s32[]{...) while((s32[]{:T(128)}, f32[2,1024]{1,0:T(2,128)S(1)}, ...), condition=%wide.region_3.4_spmd, body=%wide.region_0.3_spmd.sunk | while | flops 205853184 | bytes 8521447 | solution.py:64
  83.5 0.6 add_compare_fusion.4
  84.1 1.2 convolution_convert_fusion.4
  85.3 0.5 bitcast_reduce_fusion.4
  85.9 0.4 fusion.55
  86.3 0.6 convolution_add_fusion.4
  87.0 0.6 dynamic_slice.21
  87.6 1.9 collective-permute-start.4
  89.5 7.3 %collective-permute-start.2 = (f32[2,1024]{1,0:T(2,128)S(1)}, f32[2,1024]{1,0:T(2,128)S(1)}, u32[]{:S(2)}, u32[]{:S(2)}) collective-permute-start(f32[2,1024]{1,0:T(2,128)S(1)} %get-tuple-element.117), channel_id=1, source_target_pairs={{0,256},{256,0},{4,260},{260,4},{8,264},{264,8},{12,268},{268,12},... | collective-permute-start | bytes 24584 | tf_op jit(solution)/shard_map/ppermute | solution.py:20
  96.8 0.7 iota_compare_fusion
  97.4 36.6 %collective-permute-done.4 = f32[2,1024]{1,0:T(2,128)S(1)} collective-permute-done((f32[2,1024]{1,0:T(2,128)S(1)}, f32[2,1024]{1,0:T(2,128)S(1)}, u32[]{:S(2)}, u32[]{:S(2)}) %collective-permute-start.4) | collective-permute-done | bytes 8224 | tf_op jit(solution)/shard_map/ppermute | solution.py:20
  134.1 0.1 collective-permute-done.2
  134.2 0.0 collective-permute-done.3
  134.2 1.8 fusion.24
  136.0 0.0 reduce-scatter.2.cloned.1.call-update
  136.1 100.3 %reduce-scatter.2.cloned.1.call-done = f32[1,1024,128]{2,1,0:T(8,128)} async-done(((f32[1,1024,512]{2,1,0:T(8,128)}), f32[1,1024,128]{2,1,0:T(8,128)}) %reduce-scatter.2.cloned.1.call-update) | async-done | bytes 524304 | tf_op jit(solution)/shard_map/reduce_scatter | solution.py:102
  (28 shorter events, 0.3 us)
Async XLA Ops:
  6.5 14.6 %copy-start = (bf16[1,1024,512]{2,1,0:T(8,128)(2,1)S(1)}, bf16[1,1024,512]{2,1,0:T(8,128)(2,1)}, u32[]{:S(2)}) copy-start(bf16[1,1024,512]{2,1,0:T(8,128)(2,1)} %param.13) | copy-start | bytes 3145732
  6.5 229.8 %reduce-scatter.2.cloned.1.call-start = ((), (), s32[]{:S(2)}) async-start(), calls=%async_computation.1 | async-start | bytes 2621440 | tf_op jit(solution)/shard_map/reduce_scatter | solution.py:102
  6.5 14.6 %copy-start.3 = (bf16[512,128]{1,0:T(8,128)(2,1)S(1)}, bf16[512,128]{1,0:T(8,128)(2,1)}, u32[]{:S(2)}) copy-start(bf16[512,128]{1,0:T(8,128)(2,1)} %param.16) | copy-start | bytes 393220
  6.5 17.1 %copy-start.4 = (s32[128]{0:T(128)S(1)}, s32[128]{0:T(128)}, u32[]{:S(2)}) copy-start(s32[128]{0:T(128)} %param.14) | copy-start | bytes 1540
  6.5 19.1 %copy-start.1 = (bf16[512,128]{1,0:T(8,128)(2,1)S(1)}, bf16[512,128]{1,0:T(8,128)(2,1)}, u32[]{:S(2)}) copy-start(bf16[512,128]{1,0:T(8,128)(2,1)} %param.17) | copy-start | bytes 393220
  6.6 19.1 %copy-start.2 = (bf16[512,128]{1,0:T(8,128)(2,1)S(1)}, bf16[512,128]{1,0:T(8,128)(2,1)}, u32[]{:S(2)}) copy-start(bf16[512,128]{1,0:T(8,128)(2,1)} %param.18) | copy-start | bytes 393220
  9.7 62.0 %collective-permute-start = (bf16[8,256,512]{2,1,0:T(8,128)(2,1)}, bf16[8,256,512]{2,1,0:T(8,128)(2,1)}, u32[]{:S(2)}, u32[]{:S(2)}) collective-permute-start(bf16[8,256,512]{2,1,0:T(8,128)(2,1)} %dynamic-slice_bitcast_fusion), channel_id=1, source_target_pairs={{0,256},{256,0},{4,260},{260,4},{8,264},{264,8},{12,268},{268,12},... | collective-permute-start | bytes 6291464 | tf_op jit(solution)/shard_map/ppermute | solution.py:20
  21.7 50.0 %collective-permute-start.1 = (bf16[1024,2,64]{0,2,1:T(8,128)(2,1)S(1)}, bf16[1024,2,64]{0,2,1:T(8,128)(2,1)S(1)}, u32[]{:S(2)}, u32[]{:S(2)}) collective-permute-start(bf16[1024,2,64]{0,2,1:T(8,128)(2,1)S(1)} %bitcast.110), channel_id=1, source_target_pairs={{0,256},{256,0},{4,260},{260,4},{8,264},{264,8},{12,268},{268,12},... | collective-permute-start | bytes 786440 | tf_op jit(solution)/shard_map/ppermute | solution.py:20
  75.4 58.8 %collective-permute-start.3 = (f32[2,1024,64]{1,2,0:T(8,128)S(1)}, f32[2,1024,64]{1,2,0:T(8,128)S(1)}, u32[]{:S(2)}, u32[]{:S(2)}) collective-permute-start(f32[2,1024,64]{1,2,0:T(8,128)S(1)} %get-tuple-element.118), channel_id=1, source_target_pairs={{0,256},{256,0},{4,260},{260,4},{8,264},{264,8},{12,268},{268,12},... | collective-permute-start | bytes 1572872 | tf_op jit(solution)/shard_map/ppermute | solution.py:20
  83.5 3.5 %copy-start.6 = (s32[128]{0:T(128)S(1)}, s32[128]{0:T(128)}, u32[]{:S(2)}) copy-start(s32[128]{0:T(128)} %param.15) | copy-start | bytes 1540
  83.5 50.7 %copy-start.5 = (bf16[128,512]{1,0:T(8,128)(2,1)S(1)}, bf16[128,512]{1,0:T(8,128)(2,1)}, u32[]{:S(2)}) copy-start(bf16[128,512]{1,0:T(8,128)(2,1)} %param.19) | copy-start | bytes 393220
  87.6 46.5 %collective-permute-start.4 = (f32[2,1024]{1,0:T(2,128)S(1)}, f32[2,1024]{1,0:T(2,128)S(1)}, u32[]{:S(2)}, u32[]{:S(2)}) collective-permute-start(f32[2,1024]{1,0:T(2,128)S(1)} %get-tuple-element.120), channel_id=1, source_target_pairs={{0,256},{256,0},{4,260},{260,4},{8,264},{264,8},{12,268},{268,12},... | collective-permute-start | bytes 24584 | tf_op jit(solution)/shard_map/ppermute | solution.py:20
  89.5 44.7 %collective-permute-start.2 = (f32[2,1024]{1,0:T(2,128)S(1)}, f32[2,1024]{1,0:T(2,128)S(1)}, u32[]{:S(2)}, u32[]{:S(2)}) collective-permute-start(f32[2,1024]{1,0:T(2,128)S(1)} %get-tuple-element.117), channel_id=1, source_target_pairs={{0,256},{256,0},{4,260},{260,4},{8,264},{264,8},{12,268},{268,12},... | collective-permute-start | bytes 24584 | tf_op jit(solution)/shard_map/ppermute | solution.py:20
Sparse Core Ops, SparseCore 0:
  136.2 100.1 reduce-scatter.1
where the time goes:
time: 244 us; the launch traced here: 243 us
  waiting for transfers between devices  183 us (75%)
  starting transfers between devices  30.6 us (13%)
  between operations  15 us (6%)
  matrix products  7.04 us (3%)
  local copies, waits for them, and re-layouts  4.6 us (2%)
  other arithmetic  2.9 us (1%)
    reduce_scatter x1, waiting for transfers between devices, body(): lax.psum_scatter(term[None], 'heads', scatter_dimension=2, tiled=True)  100 us
    ppermute x5, waiting for transfers between devices, swapped(): return lax.ppermute(block, axis, route)  82.7 us
    ppermute x5, starting transfers between devices, swapped(): return lax.ppermute(block, axis, route)  30.6 us
  transfers between devices with their start and end apart: 6, of which 4 were waited for; matrix products, arithmetic and copies ran while one was open for 2% of the time, Pallas kernels for 0%

commit v1 on v0

v1 whole, which is shorter than its diff:
```python
import jax
import jax.numpy as jnp
from jax import lax
from jax.experimental import pallas as pl
from jax.experimental.pallas import tpu as pltpu
from jax.sharding import PartitionSpec as P

D = 512
HD = 64
LMAX = 4096
CMAX = 1024
GROUP = 128
TILE = 128
STEPS = CMAX // TILE
WIDE = 2 * TILE
SPAN = 2048
LOAD = 512
LOADS = LMAX // LOAD
VROWS = GROUP + 16
FOLD = 64
MESH = pl.DeviceIdType.MESH
BF = jnp.bfloat16
F32 = jnp.float32


def kernel(
    history, candidates, lengths, counts, w_query, w_key, w_value, w_out, out,
    hist, cand, wq, wkv, wo, wo_all, keys, values, query, score0, score1, top, att, done,
    load_sem, wo_send, wo_recv, send_sem, recv_sem, out_sem,
):
    user = lax.axis_index("users")
    me = lax.axis_index("heads")
    ring = lax.axis_size("heads")
    right = lax.rem(me + 1, ring)
    left = lax.rem(me + ring - 1, ring)
    across = lax.rem(me + 2, ring)

    def load(source, target, slot):
        copy = pltpu.make_async_copy(source, target, load_sem.at[slot])
        copy.start()
        return copy

    wq_copy = load(w_query, wq, 0)
    first_cand = load(candidates.at[0, pl.ds(0, WIDE)], cand.at[pl.ds(0, WIDE)], 1)
    wk_copy = load(w_key, wkv.at[:, pl.ds(0, GROUP)], 2)
    wv_copy = load(w_value, wkv.at[:, pl.ds(GROUP, GROUP)], 3)
    hist_copies = [
        load(history.at[0, pl.ds(i * LOAD, LOAD)], hist.at[pl.ds(i * LOAD, LOAD)], 6 + i)
        for i in range(LOADS)
    ]
    rest_cand = load(
        candidates.at[0, pl.ds(WIDE, CMAX - WIDE)], cand.at[pl.ds(WIDE, CMAX - WIDE)], 4
    )
    wo_copy = load(w_out, wo, 5)

    barrier = pltpu.get_barrier_semaphore()
    for peer in (left, right, across):
        pl.semaphore_signal(barrier, inc=1, device_id={"heads": peer}, device_id_type=MESH)

    length = lengths[user]
    count = counts[user]

    def make_query(step, slot):
        rows = cand[pl.ds(pl.multiple_of(step * TILE, TILE), TILE), :]
        q = (jnp.dot(rows, wq[...], preferred_element_type=F32) * HD ** (-0.5)).astype(BF)
        first = lax.broadcasted_iota(jnp.int32, (TILE, GROUP), 1) < HD
        query[slot, :TILE] = jnp.where(first, q, jnp.zeros_like(q))
        query[slot, TILE:] = jnp.where(first, jnp.zeros_like(q), q)

    def scores(q, target, start, rows, best):
        s = lax.dot_general(
            keys[start : start + rows, :], q, (((1,), (1,)), ((), ())), preferred_element_type=F32
        )
        target[start : start + rows, :] = s
        s = jnp.max(s.reshape(rows // FOLD, FOLD, WIDE), axis=0)
        return s if best is None else jnp.maximum(best, s)

    def weigh(source, start, shift, total):
        p = jnp.exp(source[start : start + SPAN, :] - shift).astype(BF)
        r = jnp.dot(values[:, start : start + SPAN], p, preferred_element_type=F32)
        return r if total is None else total + r

    def keep_top(best):
        top[...] = jnp.broadcast_to(jnp.max(best, axis=0, keepdims=True), (8, WIDE))

    wq_copy.wait()
    first_cand.wait()
    make_query(0, 0)
    make_query(1, 1)
    wk_copy.wait()
    wv_copy.wait()
    q = query[0]
    best = None
    key0 = None
    for i in range(LOADS):
        start = i * LOAD
        hist_copies[i].wait()
        kv = jnp.dot(hist[start : start + LOAD, :], wkv[...], preferred_element_type=F32)
        place = start + lax.broadcasted_iota(jnp.int32, (LOAD, GROUP), 0)
        valid = place < length
        k = kv[:, :GROUP]
        if i == 0:
            key0 = k[0:1, :]
        else:
            k = jnp.where(valid, k, key0)
        keys[start : start + LOAD, :] = k.astype(BF)
        v = jnp.where(valid, kv[:, GROUP:], 0.0)
        values[0:GROUP, start : start + LOAD] = v.T.astype(BF)
        row = lax.broadcasted_iota(jnp.int32, (VROWS - GROUP, LOAD), 0)
        place = start + lax.broadcasted_iota(jnp.int32, (VROWS - GROUP, LOAD), 1)
        ones = jnp.where((row == 0) & (place < length), 1.0, 0.0)
        values[GROUP:, start : start + LOAD] = ones.astype(BF)
        best = scores(q, score0, start, LOAD, best)
    keep_top(best)
    rest_cand.wait()
    wo_copy.wait()

    pl.semaphore_wait(barrier, 3)

    def block(peer):
        return wo.at[:, pl.ds(pl.multiple_of(peer * GROUP, GROUP), GROUP)]

    wo_sends = []
    for slot, peer in ((1, right), (2, left), (3, across)):
        copy = pltpu.make_async_remote_copy(
            src_ref=block(peer), dst_ref=wo_all.at[slot], send_sem=wo_send.at[slot],
            recv_sem=wo_recv.at[slot], device_id={"heads": peer}, device_id_type=MESH,
        )
        copy.start()
        wo_sends.append(copy)
    wo_own = pltpu.make_async_copy(block(me), wo_all.at[0], wo_send.at[0])
    wo_own.start()

    HALF = TILE // 2

    def to_right(step):
        return pltpu.make_async_remote_copy(
            src_ref=att.at[0, step], dst_ref=att.at[1, step], send_sem=send_sem.at[0, step],
            recv_sem=recv_sem.at[0, step], device_id={"heads": right}, device_id_type=MESH,
        )

    def to_left(step):
        return pltpu.make_async_remote_copy(
            src_ref=att.at[0, step], dst_ref=att.at[2, step], send_sem=send_sem.at[1, step],
            recv_sem=recv_sem.at[1, step], device_id={"heads": left}, device_id_type=MESH,
        )

    def on_right(step):
        return pltpu.make_async_remote_copy(
            src_ref=att.at[1, step, pl.ds(0, HALF)], dst_ref=att.at[3, step, pl.ds(0, HALF)],
            send_sem=send_sem.at[2, step], recv_sem=recv_sem.at[2, step],
            device_id={"heads": right}, device_id_type=MESH,
        )

    def on_left(step):
        return pltpu.make_async_remote_copy(
            src_ref=att.at[2, step, pl.ds(HALF, HALF)], dst_ref=att.at[3, step, pl.ds(HALF, HALF)],
            send_sem=send_sem.at[3, step], recv_sem=recv_sem.at[3, step],
            device_id={"heads": left}, device_id_type=MESH,
        )

    def finish(step, total):
        ones = total[GROUP : GROUP + 1]
        first = total[:HD, :TILE] / ones[:, :TILE]
        second = total[HD:GROUP, TILE:] / ones[:, TILE:]
        att[0, step] = jnp.concatenate([first, second], axis=0).T.astype(BF)

    def send(step):
        to_right(step).start()
        to_left(step).start()

    def forward(step):
        to_right(step).wait_recv()
        to_left(step).wait_recv()
        on_right(step).start()
        on_left(step).start()

    def arrived(step):
        on_right(step).wait_recv()
        on_left(step).wait_recv()

    def out_copy(step):
        return pltpu.make_async_copy(
            done.at[step], out.at[0, pl.ds(pl.multiple_of(step * TILE, TILE), TILE)], out_sem.at[step]
        )

    def project(step):
        r = jnp.dot(att[0, step], wo_all[0], preferred_element_type=F32)
        for slot in (1, 2, 3):
            r += jnp.dot(att[slot, step], wo_all[slot], preferred_element_type=F32)
        row = step * TILE + lax.broadcasted_iota(jnp.int32, (TILE, GROUP), 0)
        done[step] = jnp.where(row < count, r, 0.0)

    def tile(step, source, target, slot):
        shift = top[0:1, :]
        total = None
        best = None
        if target is not None:
            q = query[1 - slot]
        for start in range(0, LMAX, SPAN):
            if target is not None:
                best = scores(q, target, start, SPAN, best)
            total = weigh(source, start, shift, total)
        if target is not None:
            keep_top(best)
        finish(step, total)

    def exchange(step, peeled):
        send(step)

        def forward_last():
            forward(step - 1)

        def project_last():
            arrived(step - 2)
            project(step - 2)
            out_copy(step - 2).start()

        if peeled:
            forward_last()
            project_last()
        else:
            pl.when(step >= 1)(forward_last)
            pl.when(step >= 2)(project_last)

    for copy in wo_sends:
        copy.wait_recv()
    wo_own.wait()

    @pl.loop(0, STEPS // 2 - 1)
    def _(pair):
        step = 2 * pair
        tile(step, score0, score1, 0)
        make_query(step + 2, 0)
        exchange(step, False)
        tile(step + 1, score1, score0, 1)
        make_query(step + 3, 1)
        exchange(step + 1, False)

    tile(STEPS - 2, score0, score1, 0)
    exchange(STEPS - 2, True)
    tile(STEPS - 1, score1, None, 1)
    exchange(STEPS - 1, True)
    forward(STEPS - 1)
    for step in (STEPS - 2, STEPS - 1):
        arrived(step)
        project(step)
        out_copy(step).start()
    for copy in wo_sends:
        copy.wait_send()

    @pl.loop(0, STEPS)
    def _(step):
        to_right(step).wait_send()
        to_left(step).wait_send()
        on_right(step).wait_send()
        on_left(step).wait_send()
        out_copy(step).wait()


def body(history, candidates, lengths, counts, w_query, w_key, w_value, w_out):
    anywhere = pl.BlockSpec(memory_space=pl.ANY)
    scalar = pl.BlockSpec(memory_space=pltpu.SMEM)
    groups = lax.axis_size("heads")
    return pl.pallas_call(
        kernel,
        out_shape=jax.ShapeDtypeStruct((1, CMAX, GROUP), F32),
        in_specs=[anywhere, anywhere, scalar, scalar, anywhere, anywhere, anywhere, anywhere],
        out_specs=anywhere,
        scratch_shapes=[
            pltpu.VMEM((LMAX, D), BF),
            pltpu.VMEM((CMAX, D), BF),
            pltpu.VMEM((D, GROUP), BF),
            pltpu.VMEM((D, 2 * GROUP), BF),
            pltpu.VMEM((GROUP, D), BF),
            pltpu.VMEM((groups, GROUP, GROUP), BF),
            pltpu.VMEM((LMAX, GROUP), BF),
            pltpu.VMEM((VROWS, LMAX), BF),
            pltpu.VMEM((2, WIDE, GROUP), BF),
            pltpu.VMEM((LMAX, WIDE), F32),
            pltpu.VMEM((LMAX, WIDE), F32),
            pltpu.VMEM((8, WIDE), F32),
            pltpu.VMEM((groups, STEPS, TILE, GROUP), BF),
            pltpu.VMEM((STEPS, TILE, GROUP), F32),
            pltpu.SemaphoreType.DMA((6 + LOADS,)),
            pltpu.SemaphoreType.DMA((groups,)),
            pltpu.SemaphoreType.DMA((groups,)),
            pltpu.SemaphoreType.DMA((4, STEPS)),
            pltpu.SemaphoreType.DMA((4, STEPS)),
            pltpu.SemaphoreType.DMA((STEPS,)),
        ],
        compiler_params=pltpu.CompilerParams(
            collective_id=0, has_side_effects=True, vmem_limit_bytes=60 * 2**20
        ),
    )(history, candidates, lengths, counts, w_query, w_key, w_value, w_out)


def solution(mesh):
    placed = (
        P("users", None, None),
        P("users", None, None),
        P(),
        P(),
        P(None, "heads"),
        P(None, "heads"),
        P(None, "heads"),
        P("heads", None),
    )
    return jax.shard_map(
        body, mesh=mesh, in_specs=placed, out_specs=P("users", None, "heads"), check_vma=False
    )
```

time: 244 us -> 45.2 us (0.19)
  the two profiles are of different devices: /device:TPU:1 before, /device:TPU:2 now
where the time goes in v1:
time: 45.2 us; the launch traced here: 45.1 us
  Pallas kernels  43.2 us (96%)
  local copies, waits for them, and re-layouts  1.87 us (4%)
    pallas_call x1, Pallas kernels, body(): pl.pallas_call(kernel, out_shape=jax.ShapeDtypeStruct((1, CMAX, GROUP), F...  43.2 us
    unnamed x1, local copies, waits for them, and re-layouts  1.87 us

profile of v1, /device:TPU:2, one launch (start us, length us, event | category | flops | bytes accessed | tf_op | source)
XLA Modules:
  0.0 45.1 jit_solution(5944509694833700754)
XLA Ops:
  0.0 43.2 %shard_map.82 = f32[1,1024,128]{2,1,0:T(8,128)} custom-call(bf16[1,4096,512]{2,1,0:T(8,128)(2,1)} %history.1, bf16[1,1024,512]{2,1,0:T(8,128)(2,1)} %candidates.1, s32[128]{0:T(128)} %lengths.1, s32[128]{0:T(128)} %counts.1, bf16[512,128]{1,0:T(8,128)(2,1)} %w_query.1, bf16[512,128]{1,0:T(8,128)(2,1)} %w_key.1, bf16[512,128]{1,0:T(8,128)(2,1)} %w_value.1, ...), custom_call_target="tpu_custom_call" | custom-call | tf_op jit(solution)/shard_map/pallas_call | solution.py:265
  43.2 1.9 %copy.10 = f32[1,1024,128]{2,1,0:T(8,128)} copy(f32[1,1024,128]{2,1,0:T(8,128)} %shard_map.82) | data formatting | bytes 1048576

commit v2 on v0

v2 whole, which is shorter than its diff:
```python
import jax
import jax.numpy as jnp
from jax import lax
from jax.experimental import pallas as pl
from jax.experimental.pallas import tpu as pltpu
from jax.sharding import PartitionSpec as P

D = 512
HD = 64
LMAX = 4096
CMAX = 1024
GROUP = 128
TILE = 128
STEPS = CMAX // TILE
WIDE = 2 * TILE
SPAN = 512
LOADS = (512, 1024, 1024, 1024, 512)
STARTS = tuple(sum(LOADS[:i]) for i in range(len(LOADS)))
VROWS = GROUP + 16
FOLD = 64
WO_AT = 3
MESH = pl.DeviceIdType.MESH
BF = jnp.bfloat16
F32 = jnp.float32


def kernel(
    history, candidates, lengths, counts, w_query, w_key, w_value, w_out, out,
    hist, cand, wq, wkv, wo, wo_all, keys, values, score, top, att,
    length_of, count_of, load_sem, wo_send, wo_recv, send_sem, recv_sem,
):
    user = lax.axis_index("users")
    me = lax.axis_index("heads")
    ring = lax.axis_size("heads")
    right = lax.rem(me + 1, ring)
    left = lax.rem(me + ring - 1, ring)
    across = lax.rem(me + 2, ring)

    def load(source, target, slot):
        copy = pltpu.make_async_copy(source, target, load_sem.at[slot])
        copy.start()
        return copy

    def load_history(i):
        rows = pl.ds(STARTS[i], LOADS[i])
        return load(history.at[0, rows], hist.at[rows], 8 + i)

    wk_copy = load(w_key, wkv.at[:, pl.ds(0, GROUP)], 2)
    wv_copy = load(w_value, wkv.at[:, pl.ds(GROUP, GROUP)], 3)
    hist_copies = [load_history(0)]
    length_copy = load(lengths, length_of, 6)
    wq_copy = load(w_query, wq, 0)
    first_cand = load(candidates.at[0, pl.ds(0, TILE)], cand.at[pl.ds(0, TILE)], 1)
    wo_copy = load(w_out, wo, 5)
    hist_copies += [load_history(i) for i in range(1, len(LOADS))]
    count_copy = load(counts, count_of, 7)
    rest_cand = load(
        candidates.at[0, pl.ds(TILE, CMAX - TILE)], cand.at[pl.ds(TILE, CMAX - TILE)], 4
    )

    barrier = pltpu.get_barrier_semaphore()
    for peer in (left, right, across):
        pl.semaphore_signal(barrier, inc=1, device_id={"heads": peer}, device_id_type=MESH)

    def make_query(step):
        rows = cand[pl.ds(pl.multiple_of(step * TILE, TILE), TILE), :]
        q = (jnp.dot(rows, wq[...], preferred_element_type=F32) * HD ** (-0.5)).astype(BF)
        first = lax.broadcasted_iota(jnp.int32, (TILE, GROUP), 1) < HD
        zero = jnp.zeros_like(q)
        return jnp.concatenate([jnp.where(first, q, zero), jnp.where(first, zero, q)], axis=0)

    def scores(k, q, place):
        s = lax.dot_general(k, q, (((1,), (1,)), ((), ())), preferred_element_type=F32)
        score[place, :] = s
        return jnp.max(s.reshape(-1, FOLD, WIDE), axis=0)

    def keep_top(highest):
        top[...] = jnp.broadcast_to(jnp.max(highest, axis=0, keepdims=True), (8, WIDE))

    def block(peer):
        return wo.at[:, pl.ds(pl.multiple_of(peer * GROUP, GROUP), GROUP)]

    wo_own = pltpu.make_async_copy(block(me), wo_all.at[0], wo_send.at[0])
    wo_sends = [
        pltpu.make_async_remote_copy(
            src_ref=block(peer), dst_ref=wo_all.at[slot], send_sem=wo_send.at[slot],
            recv_sem=wo_recv.at[slot], device_id={"heads": peer}, device_id_type=MESH,
        )
        for slot, peer in ((3, across), (1, right), (2, left))
    ]

    def exchange_wo():
        wo_copy.wait()
        pl.semaphore_wait(barrier, 3)
        for copy in wo_sends + [wo_own]:
            copy.start()

    wk_copy.wait()
    wv_copy.wait()
    length_copy.wait()
    length = length_of[user]
    highest = None
    for i, (start, size) in enumerate(zip(STARTS, LOADS)):
        place = pl.ds(start, size)
        hist_copies[i].wait()
        kv = jnp.dot(hist[place, :], wkv[...], preferred_element_type=F32)
        valid = start + lax.broadcasted_iota(jnp.int32, (size, GROUP), 0) < length
        if i == 0:
            key0 = kv[0:1, :GROUP]
        keys[place, :] = jnp.where(valid, kv[:, :GROUP], key0).astype(BF)
        values[0:GROUP, place] = jnp.where(valid, kv[:, GROUP:], 0.0).T.astype(BF)
        row = lax.broadcasted_iota(jnp.int32, (VROWS - GROUP, size), 0)
        column = start + lax.broadcasted_iota(jnp.int32, (VROWS - GROUP, size), 1)
        ones = jnp.where((row == 0) & (column < length), 1.0, 0.0)
        values[GROUP:, place] = ones.astype(BF)
        if i == 0:
            wq_copy.wait()
            first_cand.wait()
            q = make_query(0)
        else:
            before = pl.ds(STARTS[i - 1], LOADS[i - 1])
            s = scores(keys[before, :], q, before)
            highest = s if highest is None else jnp.maximum(highest, s)
        if i == WO_AT:
            exchange_wo()
    place = pl.ds(STARTS[-1], LOADS[-1])
    keep_top(jnp.maximum(highest, scores(keys[place, :], q, place)))
    rest_cand.wait()
    count_copy.wait()
    count = count_of[user]

    def sends(step):
        return [
            pltpu.make_async_remote_copy(
                src_ref=att.at[0, step], dst_ref=att.at[slot, step],
                send_sem=send_sem.at[slot, step], recv_sem=recv_sem.at[slot, step],
                device_id={"heads": peer}, device_id_type=MESH,
            )
            for slot, peer in ((3, across), (1, right), (2, left))
        ]

    def tile(step, more):
        shift = top[0:1, :]
        total = None
        highest = None
        if more:
            q = make_query(step + 1)
        for start in range(0, LMAX, SPAN):
            place = pl.ds(start, SPAN)
            p = jnp.exp(score[place, :] - shift).astype(BF)
            r = jnp.dot(values[:, place], p, preferred_element_type=F32)
            total = r if total is None else total + r
            if more:
                s = scores(keys[place, :], q, place)
                highest = s if highest is None else jnp.maximum(highest, s)
        if more:
            keep_top(highest)
        ones = total[GROUP : GROUP + 1]
        first = total[:HD, :TILE] / ones[:, :TILE]
        second = total[HD:GROUP, TILE:] / ones[:, TILE:]
        att[0, step] = jnp.concatenate([first, second], axis=0).T.astype(BF)

    def project(step):
        r = jnp.dot(att[0, step], wo_all[0], preferred_element_type=F32)
        for slot in (1, 2, 3):
            r += jnp.dot(att[slot, step], wo_all[slot], preferred_element_type=F32)
        row = step * TILE + lax.broadcasted_iota(jnp.int32, (TILE, GROUP), 0)
        out[0, pl.ds(pl.multiple_of(step * TILE, TILE), TILE), :] = jnp.where(row < count, r, 0.0)

    @pl.loop(0, STEPS - 1)
    def _(step):
        tile(step, True)

        for copy in sends(step):
            copy.start()

    tile(STEPS - 1, False)
    for copy in sends(STEPS - 1):
        copy.start()
    wo_own.wait()
    for copy in wo_sends:
        copy.wait()

    @pl.loop(0, STEPS)
    def _(step):
        for copy in sends(step):
            copy.wait_recv()
        project(step)

    @pl.loop(0, STEPS)
    def _(step):
        for copy in sends(step):
            copy.wait_send()


def body(history, candidates, lengths, counts, w_query, w_key, w_value, w_out):
    in_hbm = pl.BlockSpec(memory_space=pltpu.HBM)
    groups = lax.axis_size("heads")
    return pl.pallas_call(
        kernel,
        out_shape=pltpu.VMEM((1, CMAX, GROUP), F32),
        in_specs=[in_hbm] * 8,
        out_specs=pl.BlockSpec(memory_space=pltpu.VMEM),
        scratch_shapes=[
            pltpu.VMEM((LMAX, D), BF),
            pltpu.VMEM((CMAX, D), BF),
            pltpu.VMEM((D, GROUP), BF),
            pltpu.VMEM((D, 2 * GROUP), BF),
            pltpu.VMEM((GROUP, D), BF),
            pltpu.VMEM((groups, GROUP, GROUP), BF),
            pltpu.VMEM((LMAX, GROUP), BF),
            pltpu.VMEM((VROWS, LMAX), BF),
            pltpu.VMEM((LMAX, WIDE), F32),
            pltpu.VMEM((8, WIDE), F32),
            pltpu.VMEM((groups, STEPS, TILE, GROUP), BF),
            pltpu.SMEM(lengths.shape, jnp.int32),
            pltpu.SMEM(counts.shape, jnp.int32),
            pltpu.SemaphoreType.DMA((8 + len(LOADS),)),
            pltpu.SemaphoreType.DMA((groups,)),
            pltpu.SemaphoreType.DMA((groups,)),
            pltpu.SemaphoreType.DMA((4, STEPS)),
            pltpu.SemaphoreType.DMA((4, STEPS)),
        ],
        compiler_params=pltpu.CompilerParams(
            collective_id=0, has_side_effects=True, vmem_limit_bytes=60 * 2**20
        ),
    )(history, candidates, lengths, counts, w_query, w_key, w_value, w_out)


def solution(mesh):
    placed = (
        P("users", None, None),
        P("users", None, None),
        P(),
        P(),
        P(None, "heads"),
        P(None, "heads"),
        P(None, "heads"),
        P("heads", None),
    )
    return jax.shard_map(
        body, mesh=mesh, in_specs=placed, out_specs=P("users", None, "heads"), check_vma=False
    )
```

time: 244 us -> 24.9 us (0.10)
  the two profiles are of different devices: /device:TPU:1 before, /device:TPU:2 now
where the time goes in v2:
time: 24.9 us; the launch traced here: 24.8 us
  Pallas kernels  24 us (96%)
  local copies, waits for them, and re-layouts  0.8 us (3%)
    pallas_call x1, Pallas kernels, body(): pl.pallas_call(kernel, out_shape=pltpu.VMEM((1, CMAX, GROUP), F32), in_sp...  24 us
    unnamed x1, local copies, waits for them, and re-layouts  0.8 us

profile of v2, /device:TPU:2, one launch (start us, length us, event | category | flops | bytes accessed | tf_op | source)
XLA Modules:
  0.0 24.8 jit_solution(10503237778744731652)
XLA Ops:
  0.0 24.0 %shard_map.82 = f32[1,1024,128]{2,1,0:T(8,128)S(1)} custom-call(bf16[1,4096,512]{2,1,0:T(8,128)(2,1)} %history.1, bf16[1,1024,512]{2,1,0:T(8,128)(2,1)} %candidates.1, s32[128]{0:T(128)} %lengths.1, s32[128]{0:T(128)} %counts.1, bf16[512,128]{1,0:T(8,128)(2,1)} %w_query.1, bf16[512,128]{1,0:T(8,128)(2,1)} %w_key.1, bf16[512,128]{1,0:T(8,128)(2,1)} %w_value.1, ...), custom_call_target="tpu_custom_call" | custom-call | tf_op jit(solution)/shard_map/pallas_call | solution.py:199
  24.0 0.8 %copy.10 = f32[1,1024,128]{2,1,0:T(8,128)} copy(f32[1,1024,128]{2,1,0:T(8,128)S(1)} %shard_map.82) | data formatting | bytes 1048576

commit v3 on v2

--- a/solution.py
+++ b/solution.py
@@ -1,3 +1,5 @@
+import functools
+
 import jax
 import jax.numpy as jnp
 from jax import lax
@@ -14,11 +16,13 @@
 STEPS = CMAX // TILE
 WIDE = 2 * TILE
 SPAN = 512
-LOADS = (512, 1024, 1024, 1024, 512)
-STARTS = tuple(sum(LOADS[:i]) for i in range(len(LOADS)))
+LOAD = 1024
+LOADS = LMAX // LOAD
 VROWS = GROUP + 16
 FOLD = 64
-WO_AT = 3
+RELAYED = range(2, 7)
+LAG = 3
+HALF = TILE // 2
 MESH = pl.DeviceIdType.MESH
 BF = jnp.bfloat16
 F32 = jnp.float32
@@ -26,7 +30,7 @@
 
 def kernel(
     history, candidates, lengths, counts, w_query, w_key, w_value, w_out, out,
-    hist, cand, wq, wkv, wo, wo_all, keys, values, score, top, att,
+    hist, cand, wq, wkv, wo, wo_all, keys, key0, values, query, best, score, top, att,
     length_of, count_of, load_sem, wo_send, wo_recv, send_sem, recv_sem,
 ):
     user = lax.axis_index("users")
@@ -42,17 +46,18 @@
         return copy
 
     def load_history(i):
-        rows = pl.ds(STARTS[i], LOADS[i])
-        return load(history.at[0, rows], hist.at[rows], 8 + i)
+        rows = pl.ds(pl.multiple_of(i * LOAD, LOAD), LOAD)
+        return pltpu.make_async_copy(history.at[0, rows], hist.at[rows], load_sem.at[8 + i])
 
     wk_copy = load(w_key, wkv.at[:, pl.ds(0, GROUP)], 2)
     wv_copy = load(w_value, wkv.at[:, pl.ds(GROUP, GROUP)], 3)
-    hist_copies = [load_history(0)]
+    load_history(0).start()
     length_copy = load(lengths, length_of, 6)
     wq_copy = load(w_query, wq, 0)
     first_cand = load(candidates.at[0, pl.ds(0, TILE)], cand.at[pl.ds(0, TILE)], 1)
     wo_copy = load(w_out, wo, 5)
-    hist_copies += [load_history(i) for i in range(1, len(LOADS))]
+    for i in range(1, LOADS):
+        load_history(i).start()
     count_copy = load(counts, count_of, 7)
     rest_cand = load(
         candidates.at[0, pl.ds(TILE, CMAX - TILE)], cand.at[pl.ds(TILE, CMAX - TILE)], 4
@@ -99,45 +104,87 @@
     wv_copy.wait()
     length_copy.wait()
     length = length_of[user]
-    highest = None
-    for i, (start, size) in enumerate(zip(STARTS, LOADS)):
-        place = pl.ds(start, size)
-        hist_copies[i].wait()
-        kv = jnp.dot(hist[place, :], wkv[...], preferred_element_type=F32)
-        valid = start + lax.broadcasted_iota(jnp.int32, (size, GROUP), 0) < length
-        if i == 0:
-            key0 = kv[0:1, :GROUP]
-        keys[place, :] = jnp.where(valid, kv[:, :GROUP], key0).astype(BF)
-        values[0:GROUP, place] = jnp.where(valid, kv[:, GROUP:], 0.0).T.astype(BF)
-        row = lax.broadcasted_iota(jnp.int32, (VROWS - GROUP, size), 0)
-        column = start + lax.broadcasted_iota(jnp.int32, (VROWS - GROUP, size), 1)
-        ones = jnp.where((row == 0) & (column < length), 1.0, 0.0)
-        values[GROUP:, place] = ones.astype(BF)
-        if i == 0:
-            wq_copy.wait()
-            first_cand.wait()
-            q = make_query(0)
-        else:
-            before = pl.ds(STARTS[i - 1], LOADS[i - 1])
-            s = scores(keys[before, :], q, before)
+    def project_history(i, first):
+        for part in range(0, LOAD, 256):
+            start = pl.multiple_of(i * LOAD + part, 256)
+            place = pl.ds(start, 256)
+            kv = jnp.dot(hist[place, :], wkv[...], preferred_element_type=F32)
+            if first and part == 0:
+                key0[...] = kv[0:8, :GROUP]
+            valid = start + lax.broadcasted_iota(jnp.int32, (256, GROUP), 0) < length
+            keys[place, :] = jnp.where(valid, kv[:, :GROUP], key0[0:1, :]).astype(BF)
+            values[0:GROUP, place] = jnp.where(valid, kv[:, GROUP:], 0.0).T.astype(BF)
+            row = lax.broadcasted_iota(jnp.int32, (VROWS - GROUP, 256), 0)
+            column = start + lax.broadcasted_iota(jnp.int32, (VROWS - GROUP, 256), 1)
+            ones = jnp.where((row == 0) & (column < length), 1.0, 0.0)
+            values[GROUP:, place] = ones.astype(BF)
+
+    def first_scores(i):
+        highest = None
+        for part in range(0, LOAD, 256):
+            place = pl.ds(pl.multiple_of(i * LOAD + part, 256), 256)
+            s = scores(keys[place, :], query[...], place)
             highest = s if highest is None else jnp.maximum(highest, s)
-        if i == WO_AT:
-            exchange_wo()
-    place = pl.ds(STARTS[-1], LOADS[-1])
-    keep_top(jnp.maximum(highest, scores(keys[place, :], q, place)))
+        return highest
+
+    load_history(0).wait()
+    project_history(0, True)
+    wq_copy.wait()
+    first_cand.wait()
+    query[...] = make_query(0)
+    best[...] = jnp.full_like(best, -jnp.inf)
+
+    @pl.loop(1, LOADS)
+    def _(i):
+        pl.when(i == LOADS - 1)(exchange_wo)
+        load_history(i).wait()
+        best[...] = jnp.maximum(best[...], first_scores(i - 1))
+        project_history(i, False)
+
+    keep_top(jnp.maximum(best[...], first_scores(LOADS - 1)))
     rest_cand.wait()
     count_copy.wait()
     count = count_of[user]
 
-    def sends(step):
-        return [
-            pltpu.make_async_remote_copy(
-                src_ref=att.at[0, step], dst_ref=att.at[slot, step],
-                send_sem=send_sem.at[slot, step], recv_sem=recv_sem.at[slot, step],
-                device_id={"heads": peer}, device_id_type=MESH,
-            )
-            for slot, peer in ((3, across), (1, right), (2, left))
-        ]
+    def remote(step, source, slot, sem, peer, rows):
+        return pltpu.make_async_remote_copy(
+            src_ref=att.at[source, step, rows], dst_ref=att.at[slot, step, rows],
+            send_sem=send_sem.at[sem, step], recv_sem=recv_sem.at[sem, step],
+            device_id={"heads": peer}, device_id_type=MESH,
+        )
+
+    def near(step):
+        whole = pl.ds(0, TILE)
+        return [remote(step, 0, 1, 1, right, whole), remote(step, 0, 2, 2, left, whole)]
+
+    def far(step):
+        return [remote(step, 0, 3, 3, across, pl.ds(0, TILE))]
+
+    def relays(step):
+        upper, lower = pl.ds(0, HALF), pl.ds(HALF, HALF)
+        return [remote(step, 1, 3, 3, right, upper), remote(step, 2, 3, 0, left, lower)]
+
+    through = lax.rem(user, 2) == 1
+
+    def start(copies):
+        for copy in copies:
+            copy.start()
+
+    def relay(step):
+        for copy in near(step):
+            copy.wait_recv()
+        start(relays(step))
+
+    def send(step):
+        @pl.when((step < RELAYED.start) | (step >= RELAYED.stop) | jnp.logical_not(through))
+        def _():
+            start(far(step))
+
+        start(near(step))
+
+        @pl.when((step >= LAG + RELAYED.start) & (step < LAG + RELAYED.stop) & through)
+        def _():
+            relay(step - LAG)
 
     def tile(step, more):
         shift = top[0:1, :]
@@ -161,36 +208,45 @@
         att[0, step] = jnp.concatenate([first, second], axis=0).T.astype(BF)
 
     def project(step):
-        r = jnp.dot(att[0, step], wo_all[0], preferred_element_type=F32)
-        for slot in (1, 2, 3):
-            r += jnp.dot(att[slot, step], wo_all[slot], preferred_element_type=F32)
+        rows = jnp.concatenate([att[slot, step] for slot in range(4)], axis=1)
+        r = jnp.dot(rows, wo_all[...].reshape(4 * GROUP, GROUP), preferred_element_type=F32)
         row = step * TILE + lax.broadcasted_iota(jnp.int32, (TILE, GROUP), 0)
         out[0, pl.ds(pl.multiple_of(step * TILE, TILE), TILE), :] = jnp.where(row < count, r, 0.0)
 
     @pl.loop(0, STEPS - 1)
     def _(step):
         tile(step, True)
-
-        for copy in sends(step):
-            copy.start()
+        send(step)
 
     tile(STEPS - 1, False)
-    for copy in sends(STEPS - 1):
-        copy.start()
+    send(STEPS - 1)
     wo_own.wait()
     for copy in wo_sends:
         copy.wait()
-
-    @pl.loop(0, STEPS)
-    def _(step):
-        for copy in sends(step):
-            copy.wait_recv()
+    late = range(STEPS - LAG, RELAYED.stop)
+    for step in late:
+        pl.when(through)(functools.partial(relay, step))
+    for step in range(STEPS):
+        if step in RELAYED:
+            for copy in near(step):
+                copy.wait_send()
+
+            @pl.when(through)
+            def _():
+                for copy in relays(step):
+                    copy.wait()
+
+            @pl.when(jnp.logical_not(through))
+            def _():
+                for copy in near(step):
+                    copy.wait_recv()
+                for copy in far(step):
+                    copy.wait()
+
+        else:
+            for copy in far(step) + near(step):
+                copy.wait()
         project(step)
-
-    @pl.loop(0, STEPS)
-    def _(step):
-        for copy in sends(step):
-            copy.wait_send()
 
 
 def body(history, candidates, lengths, counts, w_query, w_key, w_value, w_out):
@@ -209,13 +265,16 @@
             pltpu.VMEM((GROUP, D), BF),
             pltpu.VMEM((groups, GROUP, GROUP), BF),
             pltpu.VMEM((LMAX, GROUP), BF),
+            pltpu.VMEM((8, GROUP), F32),
             pltpu.VMEM((VROWS, LMAX), BF),
+            pltpu.VMEM((WIDE, GROUP), BF),
+            pltpu.VMEM((FOLD, WIDE), F32),
             pltpu.VMEM((LMAX, WIDE), F32),
             pltpu.VMEM((8, WIDE), F32),
             pltpu.VMEM((groups, STEPS, TILE, GROUP), BF),
             pltpu.SMEM(lengths.shape, jnp.int32),
             pltpu.SMEM(counts.shape, jnp.int32),
-            pltpu.SemaphoreType.DMA((8 + len(LOADS),)),
+            pltpu.SemaphoreType.DMA((8 + LOADS,)),
             pltpu.SemaphoreType.DMA((groups,)),
             pltpu.SemaphoreType.DMA((groups,)),
             pltpu.SemaphoreType.DMA((4, STEPS)),

time: 24.9 us -> 24.5 us (0.984)
  Pallas kernels: 24 us -> 23.6 us
    pallas_call x1, Pallas kernels: 24 us -> 23.6 us  [body(): pl.pallas_call(kernel, out_shape=pltpu.VMEM((1, CMAX, GROUP), F32), in_sp...]
where the time goes in v3:
time: 24.5 us; the launch traced here: 24.4 us
  Pallas kernels  23.6 us (96%)
  local copies, waits for them, and re-layouts  0.8 us (3%)
    pallas_call x1, Pallas kernels, body(): pl.pallas_call(kernel, out_shape=pltpu.VMEM((1, CMAX, GROUP), F32), in_sp...  23.6 us
    unnamed x1, local copies, waits for them, and re-layouts  0.8 us

profile of v3, /device:TPU:2, one launch (start us, length us, event | category | flops | bytes accessed | tf_op | source)
XLA Modules:
  0.0 24.4 jit_solution(17847210114242941415)
XLA Ops:
  0.0 23.6 %shard_map.82 = f32[1,1024,128]{2,1,0:T(8,128)S(1)} custom-call(bf16[1,4096,512]{2,1,0:T(8,128)(2,1)} %history.1, bf16[1,1024,512]{2,1,0:T(8,128)(2,1)} %candidates.1, s32[128]{0:T(128)} %lengths.1, s32[128]{0:T(128)} %counts.1, bf16[512,128]{1,0:T(8,128)(2,1)} %w_query.1, bf16[512,128]{1,0:T(8,128)(2,1)} %w_key.1, bf16[512,128]{1,0:T(8,128)(2,1)} %w_value.1, ...), custom_call_target="tpu_custom_call" | custom-call | tf_op jit(solution)/shard_map/pallas_call | solution.py:255
  23.6 0.8 %copy.10 = f32[1,1024,128]{2,1,0:T(8,128)} copy(f32[1,1024,128]{2,1,0:T(8,128)S(1)} %shard_map.82) | data formatting | bytes 1048576

commit v4 on v3

--- a/solution.py
+++ b/solution.py
@@ -16,8 +16,8 @@
 STEPS = CMAX // TILE
 WIDE = 2 * TILE
 SPAN = 512
-LOAD = 1024
-LOADS = LMAX // LOAD
+LOADS = (1024, 1024, 2048)
+STARTS = tuple(sum(LOADS[:i]) for i in range(len(LOADS)))
 VROWS = GROUP + 16
 FOLD = 64
 RELAYED = range(2, 7)
@@ -30,7 +30,7 @@
 
 def kernel(
     history, candidates, lengths, counts, w_query, w_key, w_value, w_out, out,
-    hist, cand, wq, wkv, wo, wo_all, keys, key0, values, query, best, score, top, att,
+    hist, cand, wq, wkv, wo, wo_all, keys, key0, values, query, score, top, att,
     length_of, count_of, load_sem, wo_send, wo_recv, send_sem, recv_sem,
 ):
     user = lax.axis_index("users")
@@ -46,7 +46,7 @@
         return copy
 
     def load_history(i):
-        rows = pl.ds(pl.multiple_of(i * LOAD, LOAD), LOAD)
+        rows = pl.ds(STARTS[i], LOADS[i])
         return pltpu.make_async_copy(history.at[0, rows], hist.at[rows], load_sem.at[8 + i])
 
     wk_copy = load(w_key, wkv.at[:, pl.ds(0, GROUP)], 2)
@@ -56,7 +56,7 @@
     wq_copy = load(w_query, wq, 0)
     first_cand = load(candidates.at[0, pl.ds(0, TILE)], cand.at[pl.ds(0, TILE)], 1)
     wo_copy = load(w_out, wo, 5)
-    for i in range(1, LOADS):
+    for i in range(1, len(LOADS)):
         load_history(i).start()
     count_copy = load(counts, count_of, 7)
     rest_cand = load(
@@ -104,12 +104,11 @@
     wv_copy.wait()
     length_copy.wait()
     length = length_of[user]
-    def project_history(i, first):
-        for part in range(0, LOAD, 256):
-            start = pl.multiple_of(i * LOAD + part, 256)
+    def project_history(i):
+        for start in range(STARTS[i], STARTS[i] + LOADS[i], 256):
             place = pl.ds(start, 256)
             kv = jnp.dot(hist[place, :], wkv[...], preferred_element_type=F32)
-            if first and part == 0:
+            if start == 0:
                 key0[...] = kv[0:8, :GROUP]
             valid = start + lax.broadcasted_iota(jnp.int32, (256, GROUP), 0) < length
             keys[place, :] = jnp.where(valid, kv[:, :GROUP], key0[0:1, :]).astype(BF)
@@ -121,28 +120,28 @@
 
     def first_scores(i):
         highest = None
-        for part in range(0, LOAD, 256):
-            place = pl.ds(pl.multiple_of(i * LOAD + part, 256), 256)
-            s = scores(keys[place, :], query[...], place)
+        for start in range(STARTS[i], STARTS[i] + LOADS[i], 256):
+            place = pl.ds(start, 256)
+            s = scores(keys[place, :], q, place)
             highest = s if highest is None else jnp.maximum(highest, s)
         return highest
 
     load_history(0).wait()
-    project_history(0, True)
+    project_history(0)
     wq_copy.wait()
     first_cand.wait()
-    query[...] = make_query(0)
-    best[...] = jnp.full_like(best, -jnp.inf)
-
-    @pl.loop(1, LOADS)
-    def _(i):
-        pl.when(i == LOADS - 1)(exchange_wo)
+    q = make_query(0)
+    highest = None
+    for i in range(1, len(LOADS)):
+        if i == 2:
+            exchange_wo()
         load_history(i).wait()
-        best[...] = jnp.maximum(best[...], first_scores(i - 1))
-        project_history(i, False)
-
-    keep_top(jnp.maximum(best[...], first_scores(LOADS - 1)))
+        s = first_scores(i - 1)
+        highest = s if highest is None else jnp.maximum(highest, s)
+        project_history(i)
+    keep_top(jnp.maximum(highest, first_scores(len(LOADS) - 1)))
     rest_cand.wait()
+    query[...] = make_query(1)
     count_copy.wait()
     count = count_of[user]
 
@@ -191,15 +190,19 @@
         total = None
         highest = None
         if more:
-            q = make_query(step + 1)
+            q = query[...]
+            query[...] = make_query(lax.rem(step + 2, STEPS))
         for start in range(0, LMAX, SPAN):
             place = pl.ds(start, SPAN)
             p = jnp.exp(score[place, :] - shift).astype(BF)
             r = jnp.dot(values[:, place], p, preferred_element_type=F32)
             total = r if total is None else total + r
             if more:
-                s = scores(keys[place, :], q, place)
-                highest = s if highest is None else jnp.maximum(highest, s)
+                size = SPAN // 2
+                for part in range(start, start + SPAN, size):
+                    place = pl.ds(part, size)
+                    s = scores(keys[place, :], q, place)
+                    highest = s if highest is None else jnp.maximum(highest, s)
         if more:
             keep_top(highest)
         ones = total[GROUP : GROUP + 1]
@@ -268,13 +271,12 @@
             pltpu.VMEM((8, GROUP), F32),
             pltpu.VMEM((VROWS, LMAX), BF),
             pltpu.VMEM((WIDE, GROUP), BF),
-            pltpu.VMEM((FOLD, WIDE), F32),
             pltpu.VMEM((LMAX, WIDE), F32),
             pltpu.VMEM((8, WIDE), F32),
             pltpu.VMEM((groups, STEPS, TILE, GROUP), BF),
             pltpu.SMEM(lengths.shape, jnp.int32),
             pltpu.SMEM(counts.shape, jnp.int32),
-            pltpu.SemaphoreType.DMA((8 + LOADS,)),
+            pltpu.SemaphoreType.DMA((8 + len(LOADS),)),
             pltpu.SemaphoreType.DMA((groups,)),
             pltpu.SemaphoreType.DMA((groups,)),
             pltpu.SemaphoreType.DMA((4, STEPS)),

time: 24.5 us -> 23.6 us (0.963)
  Pallas kernels: 23.6 us -> 22.7 us
    pallas_call x1, Pallas kernels: 23.6 us -> 22.7 us  [body(): pl.pallas_call(kernel, out_shape=pltpu.VMEM((1, CMAX, GROUP), F32), in_sp...]
where the time goes in v4:
time: 23.6 us; the launch traced here: 23.5 us
  Pallas kernels  22.7 us (96%)
  local copies, waits for them, and re-layouts  0.8 us (3%)
    pallas_call x1, Pallas kernels, body(): pl.pallas_call(kernel, out_shape=pltpu.VMEM((1, CMAX, GROUP), F32), in_sp...  22.7 us
    unnamed x1, local copies, waits for them, and re-layouts  0.8 us

profile of v4, /device:TPU:2, one launch (start us, length us, event | category | flops | bytes accessed | tf_op | source)
XLA Modules:
  0.0 23.5 jit_solution(3893808608143567069)
XLA Ops:
  0.0 22.7 %shard_map.82 = f32[1,1024,128]{2,1,0:T(8,128)S(1)} custom-call(bf16[1,4096,512]{2,1,0:T(8,128)(2,1)} %history.1, bf16[1,1024,512]{2,1,0:T(8,128)(2,1)} %candidates.1, s32[128]{0:T(128)} %lengths.1, s32[128]{0:T(128)} %counts.1, bf16[512,128]{1,0:T(8,128)(2,1)} %w_query.1, bf16[512,128]{1,0:T(8,128)(2,1)} %w_key.1, bf16[512,128]{1,0:T(8,128)(2,1)} %w_value.1, ...), custom_call_target="tpu_custom_call" | custom-call | tf_op jit(solution)/shard_map/pallas_call | solution.py:258
  22.7 0.8 %copy.10 = f32[1,1024,128]{2,1,0:T(8,128)} copy(f32[1,1024,128]{2,1,0:T(8,128)S(1)} %shard_map.82) | data formatting | bytes 1048576

commit v5 on v4

--- a/solution.py
+++ b/solution.py
@@ -21,7 +21,7 @@
 VROWS = GROUP + 16
 FOLD = 64
 RELAYED = range(2, 7)
-LAG = 3
+LAG = 4
 HALF = TILE // 2
 MESH = pl.DeviceIdType.MESH
 BF = jnp.bfloat16

time: 23.6 us -> 23.6 us (level)
  no operation moved by 1% of the time
where the time goes in v5:
time: 23.6 us; the launch traced here: 23.5 us
  Pallas kernels  22.7 us (96%)
  local copies, waits for them, and re-layouts  0.8 us (3%)
    pallas_call x1, Pallas kernels, body(): pl.pallas_call(kernel, out_shape=pltpu.VMEM((1, CMAX, GROUP), F32), in_sp...  22.7 us
    unnamed x1, local copies, waits for them, and re-layouts  0.8 us

profile of v5, /device:TPU:2, one launch (start us, length us, event | category | flops | bytes accessed | tf_op | source)
XLA Modules:
  0.0 23.5 jit_solution(13176627743138588401)
XLA Ops:
  0.0 22.7 %shard_map.82 = f32[1,1024,128]{2,1,0:T(8,128)S(1)} custom-call(bf16[1,4096,512]{2,1,0:T(8,128)(2,1)} %history.1, bf16[1,1024,512]{2,1,0:T(8,128)(2,1)} %candidates.1, s32[128]{0:T(128)} %lengths.1, s32[128]{0:T(128)} %counts.1, bf16[512,128]{1,0:T(8,128)(2,1)} %w_query.1, bf16[512,128]{1,0:T(8,128)(2,1)} %w_key.1, bf16[512,128]{1,0:T(8,128)(2,1)} %w_value.1, ...), custom_call_target="tpu_custom_call" | custom-call | tf_op jit(solution)/shard_map/pallas_call | solution.py:258
  22.7 0.8 %copy.10 = f32[1,1024,128]{2,1,0:T(8,128)} copy(f32[1,1024,128]{2,1,0:T(8,128)S(1)} %shard_map.82) | data formatting | bytes 1048576

commit v6 on v5

--- a/solution.py
+++ b/solution.py
@@ -16,10 +16,11 @@
 STEPS = CMAX // TILE
 WIDE = 2 * TILE
 SPAN = 512
+LAST_SPAN = 1024
 LOADS = (1024, 1024, 2048)
 STARTS = tuple(sum(LOADS[:i]) for i in range(len(LOADS)))
 VROWS = GROUP + 16
-FOLD = 64
+FOLD = 32
 RELAYED = range(2, 7)
 LAG = 4
 HALF = TILE // 2
@@ -192,8 +193,9 @@
         if more:
             q = query[...]
             query[...] = make_query(lax.rem(step + 2, STEPS))
-        for start in range(0, LMAX, SPAN):
-            place = pl.ds(start, SPAN)
+        span = SPAN if more else LAST_SPAN
+        for start in range(0, LMAX, span):
+            place = pl.ds(start, span)
             p = jnp.exp(score[place, :] - shift).astype(BF)
             r = jnp.dot(values[:, place], p, preferred_element_type=F32)
             total = r if total is None else total + r

time: 23.6 us -> 23.5 us (level)
  no operation moved by 1% of the time
where the time goes in v6:
time: 23.5 us; the launch traced here: 23.4 us
  Pallas kernels  22.6 us (96%)
  local copies, waits for them, and re-layouts  0.8 us (3%)
    pallas_call x1, Pallas kernels, body(): pl.pallas_call(kernel, out_shape=pltpu.VMEM((1, CMAX, GROUP), F32), in_sp...  22.6 us
    unnamed x1, local copies, waits for them, and re-layouts  0.8 us

profile of v6, /device:TPU:2, one launch (start us, length us, event | category | flops | bytes accessed | tf_op | source)
XLA Modules:
  0.0 23.4 jit_solution(4551873711689633347)
XLA Ops:
  0.0 22.6 %shard_map.82 = f32[1,1024,128]{2,1,0:T(8,128)S(1)} custom-call(bf16[1,4096,512]{2,1,0:T(8,128)(2,1)} %history.1, bf16[1,1024,512]{2,1,0:T(8,128)(2,1)} %candidates.1, s32[128]{0:T(128)} %lengths.1, s32[128]{0:T(128)} %counts.1, bf16[512,128]{1,0:T(8,128)(2,1)} %w_query.1, bf16[512,128]{1,0:T(8,128)(2,1)} %w_key.1, bf16[512,128]{1,0:T(8,128)(2,1)} %w_value.1, ...), custom_call_target="tpu_custom_call" | custom-call | tf_op jit(solution)/shard_map/pallas_call | solution.py:260
  22.6 0.8 %copy.10 = f32[1,1024,128]{2,1,0:T(8,128)} copy(f32[1,1024,128]{2,1,0:T(8,128)S(1)} %shard_map.82) | data formatting | bytes 1048576
